TPU v7x, 512 devices: a whole 4x8x8 slice. The times are simulated.
512 devices in a mesh: sta: 64 (over y, z_hi, core), band: 8 (over x, z_lo).
Axes of the slice: x: 4, y: 8, z: 8 (z_hi: 4, z_lo: 2; z = z_hi * 2 + z_lo), core: 2. Of those that a mesh axis runs over, the one named last changes fastest.
Arguments:
- traces: bfloat16 [256, 32, 16384], P('sta', 'band'), may hold values from -400 to 400, as said below
- live_flag: int32 [256, 32], P('sta'), may hold values 0 or 1
- response: float32 [8192], P('band'), may hold values from 0.3 to 3
Outputs:
- own_cross: bfloat16 [2, 256, 4, 8192], P(None, 'sta', None, 'band')
- near_cross: bfloat16 [2, 256, 4, 8192], P(None, 'sta', None, 'band')
- far_cross: bfloat16 [2, 256, 4, 8192], P(None, 'sta', None, 'band')
Inputs may be any that keep to these rules, and one draw needn't show every extreme that they name: `traces`: recorded ground motion of each station and window.
All inputs are finite; a program needn't handle non-finite values. No bound on the sum of `live_flag` on one device may be relied on, other than what follows from the above.
Results may differ from a plain program's by a relative error of at most 0.008.
Values may be sent and summed in bfloat16 or wider, within the bound.
A program may use at most 64 MiB of HBM per device.

v0:
```python
import math

import jax
import jax.numpy as jnp
from jax import lax
from jax.sharding import PartitionSpec as P

ROOT = 128
SMOOTH = 64


epsilon = 1e-06
full_turn = 2.0 * math.pi


def padded(cells, sides, width):
    for axis, dim in sides:
        count = lax.axis_size(axis)
        ends = count - 1
        head = lax.slice_in_dim(cells, 0, width, axis=dim)
        tail = lax.slice_in_dim(cells, cells.shape[dim] - width, cells.shape[dim], axis=dim)
        cells = jnp.concatenate(
            [
                lax.ppermute(tail, axis, [(i, (i + 1) % count) for i in range(ends)]),
                cells,
                lax.ppermute(head, axis, [((i + 1) % count, i) for i in range(ends)]),
            ],
            axis=dim,
        )
    return cells


def passed_along(block, axis, distance):
    devices = range(lax.axis_size(axis))
    route = [((i - distance) % len(devices), i) for i in devices]
    return lax.ppermute(block, axis, route)


def make_tables():
    indices = jnp.arange(ROOT, dtype=jnp.int32)
    products = indices[:, None] * indices[None, :] % ROOT
    angles = products.astype(jnp.float32) * (full_turn / ROOT)
    first_table = jnp.concatenate([jnp.cos(angles), -jnp.sin(angles)], axis=1).astype(jnp.bfloat16)
    twist_angle = (indices[:, None] * indices[None, :]).astype(jnp.float32) * (
        full_turn / (ROOT * ROOT)
    )
    twist_cos = jnp.cos(twist_angle)
    twist_sin = jnp.sin(twist_angle)
    half_angle = angles[:, : ROOT // 2]
    cos_part = jnp.cos(half_angle)
    sin_part = jnp.sin(half_angle)
    second_table = jnp.stack(
        [jnp.stack([cos_part, -sin_part], axis=1), jnp.stack([sin_part, cos_part], axis=1)], axis=0
    ).astype(jnp.bfloat16)
    return (first_table, twist_cos, twist_sin, second_table)


def transform(block):
    first_table, twist_cos, twist_sin, second_table = make_tables()
    station_rows, window_rows = (block.shape[0], block.shape[1])
    folded = block.reshape(station_rows, window_rows, ROOT, ROOT)
    section_one = jnp.einsum(
        "swab,ak->swbk", folded, first_table, preferred_element_type=jnp.float32
    )
    real_one = section_one[..., :ROOT]
    imag_one = section_one[..., ROOT:]
    real_two = real_one * twist_cos + imag_one * twist_sin
    imag_two = imag_one * twist_cos - real_one * twist_sin
    twisted = jnp.stack([real_two, imag_two], axis=2).astype(jnp.bfloat16)
    result = jnp.einsum(
        "swcbk,cbeq->sweqk", twisted, second_table, preferred_element_type=jnp.float32
    )
    return result.astype(jnp.bfloat16).reshape(station_rows, window_rows, 2, ROOT // 2 * ROOT)


def cross_spectra(left, right):
    turned = jnp.stack([-right[:, :, 1], right[:, :, 0]], axis=2)
    stacked = jnp.stack([right, turned], axis=0)
    result = jnp.einsum("iwcf,ejwcf->eijf", left, stacked, preferred_element_type=jnp.float32)
    return (result / left.shape[1]).astype(jnp.bfloat16)


def local(traces, live_flag, response):
    spectra = transform(traces)
    station_rows, window_rows = (spectra.shape[0], spectra.shape[1])
    band_count = lax.axis_size("band")
    band_bins = spectra.shape[3] // band_count
    outgoing = spectra.reshape(station_rows, window_rows, 2, band_count, band_bins)
    received = lax.all_to_all(outgoing, "band", split_axis=3, concat_axis=1, tiled=True)
    received = received.reshape(station_rows, received.shape[1], 2, received.shape[4])
    windows = received.shape[1]
    window_gates = live_flag.astype(jnp.float32)
    masked = received.astype(jnp.float32) * window_gates[:, :, None, None]
    power_sum = jnp.sum(masked[:, :, 0, :] ** 2 + masked[:, :, 1, :] ** 2, axis=1)
    extended = padded(power_sum, (("band", 1),), SMOOTH)
    source_bins = jnp.arange(band_bins + 2 * SMOOTH, dtype=jnp.int32)[:, None]
    target_bins = jnp.arange(band_bins, dtype=jnp.int32)[None, :]
    distance = source_bins - target_bins
    band_matrix = ((distance >= 0) & (distance <= 2 * SMOOTH)).astype(jnp.float32)
    smooth = jnp.dot(extended, band_matrix, precision=lax.Precision.HIGHEST) / (
        (2 * SMOOTH + 1) * windows
    )
    scales = response[None, :] / jnp.sqrt(smooth + epsilon)
    whitened = (masked * scales[:, None, None, :]).astype(jnp.bfloat16)
    offset = lax.axis_size("sta") // 8
    partner_near = passed_along(whitened, "sta", -offset)
    partner_far = passed_along(whitened, "sta", -2 * offset)
    return (
        cross_spectra(whitened, whitened),
        cross_spectra(whitened, partner_near),
        cross_spectra(whitened, partner_far),
    )


def solution(mesh):
    in_specs = (P("sta", "band", None), P("sta", None), P("band"))
    out_specs = (
        P(None, "sta", None, "band"),
        P(None, "sta", None, "band"),
        P(None, "sta", None, "band"),
    )
    return jax.shard_map(local, mesh=mesh, in_specs=in_specs, out_specs=out_specs, check_vma=False)
```

profile of v0, /device:TPU:56, one launch (start us, length us, event | category | flops | bytes accessed | tf_op | source)
XLA Modules:
  0.0 101.8 jit_solution(15846620016048100098)
XLA Ops:
  0.6 0.3 negate_convert_fusion
  0.9 0.3 fusion.40
  1.2 1.6 %reshape.69 = bf16[4,4,128,128]{3,2,1,0:T(8,128)(2,1)S(1)} reshape(bf16[4,4,16384]{2,1,0:T(4,128)(2,1)} %param.3) | data formatting | bytes 1048576 | tf_op jit(solution)/shard_map/reshape | solution.py:61
  2.8 0.1 fusion.48
  2.9 0.4 convolution_bitcast_fusion
  3.4 0.3 fusion.30
  3.7 0.5 fusion.14
  4.2 0.2 reshape_reshape.3
  4.4 1.3 %copy.117 = bf16[4,4,2,8,1024]{4,2,1,0,3:T(2,128)(2,1)} copy(bf16[4,4,2,8,1024]{4,3,1,0,2:T(8,128)(2,1)S(1)} %reshape_reshape.3) | data formatting | bytes 1048576 | tf_op jit(solution)/shard_map/reshape;reshape | solution.py:88
  5.8 6.2 %all-to-all-start = ((bf16[4,4,2,8,1024]{4,2,1,0,3:T(2,128)(2,1)}), bf16[4,4,2,8,1024]{4,2,1,0,3:T(2,128)(2,1)S(1)}, u32[]{:S(2)}, u32[]{:S(2)}) async-start(bf16[4,4,2,8,1024]{4,2,1,0,3:T(2,128)(2,1)} %copy.117), calls=%async_computation | async-start | bytes 1048576 | tf_op jit(solution)/shard_map/all_to_all | solution.py:89
  12.0 10.1 %all-to-all-done = bf16[4,4,2,8,1024]{4,2,1,0,3:T(2,128)(2,1)S(1)} async-done(((bf16[4,4,2,8,1024]{4,2,1,0,3:T(2,128)(2,1)}), bf16[4,4,2,8,1024]{4,2,1,0,3:T(2,128)(2,1)S(1)}, u32[]{:S(2)}, u32[]{:S(2)}) %all-to-all-start) | async-done | bytes 524320 | tf_op jit(solution)/shard_map/all_to_all | solution.py:89
  22.1 0.4 convert_bitcast_fusion
  22.5 0.1 copy.118
  22.6 0.3 copy_multiply_fusion
  22.9 0.1 fusion.33
  23.1 0.1 fusion.52
  23.1 0.1 copy.156
  23.2 2.8 %collective-permute-start = (f32[4,64]{0,1:T(8,128)S(1)}, f32[4,64]{0,1:T(8,128)S(1)}, u32[]{:S(2)}, u32[]{:S(2)}) collective-permute-start(f32[4,64]{0,1:T(8,128)S(1)} %copy.156), channel_id=1, source_target_pairs={{0,1},{1,2},{2,3},{3,4},{4,5},{5,6},{6,7},{8,9},{9,10},{10,11},{11... | collective-permute-start | bytes 3080 | tf_op jit(solution)/shard_map/ppermute | solution.py:24
  26.0 0.1 copy.157
  26.1 1.3 %collective-permute-start.1 = (f32[4,64]{0,1:T(8,128)S(1)}, f32[4,64]{0,1:T(8,128)S(1)}, u32[]{:S(2)}, u32[]{:S(2)}) collective-permute-start(f32[4,64]{0,1:T(8,128)S(1)} %copy.157), channel_id=1, source_target_pairs={{1,0},{2,1},{3,2},{4,3},{5,4},{6,5},{7,6},{9,8},{10,9},{11,10},{12... | collective-permute-start | bytes 3080 | tf_op jit(solution)/shard_map/ppermute | solution.py:26
  27.4 0.2 collective-permute-done
  27.6 0.1 copy.123
  27.7 4.2 %collective-permute-done.1 = f32[4,64]{0,1:T(8,128)S(1)} collective-permute-done((f32[4,64]{0,1:T(8,128)S(1)}, f32[4,64]{0,1:T(8,128)S(1)}, u32[]{:S(2)}, u32[]{:S(2)}) %collective-permute-start.1) | collective-permute-done | bytes 1056 | tf_op jit(solution)/shard_map/ppermute | solution.py:26
  31.9 0.1 copy.125
  32.0 0.1 concatenate.8
  32.1 0.6 fusion.24
  32.7 1.1 %multiply_convert_fusion = bf16[4,32,2,1024]{3,1,2,0:T(8,128)(2,1)} fusion(f32[4,1024]{1,0:T(4,128)S(1)} %fusion.24, f32[4,32]{1,0:T(4,128)S(1)} %convert_element_type.106, f32[4,32,2,1024]{3,2,1,0:T(2,128)S(1)} %bitcast.97), kind=kLoop, calls=%fused_computation.34 | loop fusion | flops 786432 | bytes 1589760 | tf_op jit(solution)/shard_map/convert_element_type | solution.py:104
  33.9 0.3 fusion.61
  34.2 1.1 %slice_negate_fusion.2 = (bf16[4,32,1,1024]{3,1,2,0:T(8,128)(2,1)S(1)}, bf16[4,32,1,1024]{3,1,2,0:T(8,128)(2,1)S(1)}) fusion(bf16[4,32,2,1024]{3,1,2,0:T(8,128)(2,1)} %multiply_convert_fusion), kind=kLoop, calls=%fused_computation.48 | loop fusion | flops 131072 | bytes 1048576 | tf_op jit(solution)/shard_map/neg | solution.py:77
  35.3 3.3 %collective-permute-start.2 = (bf16[4,32,2,1024]{3,1,2,0:T(8,128)(2,1)}, bf16[4,32,2,1024]{3,1,2,0:T(8,128)(2,1)S(1)}, u32[]{:S(2)}, u32[]{:S(2)}) collective-permute-start(bf16[4,32,2,1024]{3,1,2,0:T(8,128)(2,1)} %multiply_convert_fusion), channel_id=1, source_target_pairs={{64,0},{72,8},{80,16},{88,24},{96,32},{104,40},{112,48},{120,56},{... | collective-permute-start | bytes 1572872 | tf_op jit(solution)/shard_map/ppermute | solution.py:36
  38.5 4.2 %collective-permute-start.3 = (bf16[4,32,2,1024]{3,1,2,0:T(8,128)(2,1)}, bf16[4,32,2,1024]{3,1,2,0:T(8,128)(2,1)}, u32[]{:S(2)}, u32[]{:S(2)}) collective-permute-start(bf16[4,32,2,1024]{3,1,2,0:T(8,128)(2,1)} %multiply_convert_fusion), channel_id=1, source_target_pairs={{128,0},{136,8},{144,16},{152,24},{160,32},{168,40},{176,48},{184,... | collective-permute-start | bytes 1572872 | tf_op jit(solution)/shard_map/ppermute | solution.py:36
  42.8 0.3 fusion.29
  43.2 0.1 pad_maximum_fusion
  43.3 5.4 %copy.126 = bf16[2,4,32,2,1024]{2,1,3,0,4:T(4,128)(2,1)} copy(bf16[2,4,32,2,1024]{4,2,3,1,0:T(8,128)(2,1)S(1)} %pad_maximum_fusion) | data formatting | bytes 2097152 | tf_op jit(solution)/shard_map/stack | solution.py:78
  48.7 1.4 %copy.139 = bf16[4,32,2,1024,1]{1,0,2,4,3:T(4,128)(2,1)S(1)} copy(bf16[4,32,2,1024,1]{3,1,2,0,4:T(8,128)(2,1)S(1)} %fusion.61) | data formatting | bytes 1048576 | tf_op jit(solution)/shard_map/convert_element_type | solution.py:104
  50.1 7.0 %fusion.10 = bf16[2,4,4,1024]{1,2,0,3:T(4,128)(2,1)} fusion(bf16[2,4,32,2,1024]{2,1,3,0,4:T(4,128)(2,1)} %copy.126, bf16[4,32,2,1024,1]{1,0,2,4,3:T(4,128)(2,1)S(1)} %copy.139), kind=kOutput, calls=%fused_computation.13 | convolution fusion | flops 4259840 | bytes 1638400 | tf_op jit(solution)/shard_map/iwcf,ejwcf->eijf/dot_general | solution.py:79
  57.1 4.1 %copy.132 = bf16[2,4,4,1024]{3,2,1,0:T(4,128)(2,1)} copy(bf16[2,4,4,1024]{1,2,0,3:T(4,128)(2,1)} %fusion.10) | data formatting | bytes 131072
  61.2 3.5 %collective-permute-done.2 = bf16[4,32,2,1024]{3,1,2,0:T(8,128)(2,1)S(1)} collective-permute-done((bf16[4,32,2,1024]{3,1,2,0:T(8,128)(2,1)}, bf16[4,32,2,1024]{3,1,2,0:T(8,128)(2,1)S(1)}, u32[]{:S(2)}, u32[]{:S(2)}) %collective-permute-start.2) | collective-permute-done | bytes 524320 | tf_op jit(solution)/shard_map/ppermute | solution.py:36
  64.7 0.7 copy-done
  65.4 1.1 %pad_maximum_fusion.1 = bf16[2,4,32,2,1024]{4,2,3,1,0:T(8,128)(2,1)S(1)} fusion(bf16[1,4,32,2,1024]{4,2,3,1,0:T(8,128)(2,1)S(1)} %maximum_bitcast_fusion.2, bf16[1,4,32,2,1024]{4,2,3,1,0:T(8,128)(2,1)} %bitcast.100), kind=kLoop, calls=%fused_computation.26 | loop fusion | flops 524288 | bytes 2097152 | tf_op jit(solution)/shard_map/stack | solution.py:78
  66.5 5.4 %copy.128 = bf16[2,4,32,2,1024]{2,1,3,0,4:T(4,128)(2,1)} copy(bf16[2,4,32,2,1024]{4,2,3,1,0:T(8,128)(2,1)S(1)} %pad_maximum_fusion.1) | data formatting | bytes 2097152 | tf_op jit(solution)/shard_map/stack | solution.py:78
  71.9 7.0 %fusion.11 = bf16[2,4,4,1024]{1,2,0,3:T(4,128)(2,1)} fusion(bf16[2,4,32,2,1024]{2,1,3,0,4:T(4,128)(2,1)} %copy.128, bf16[4,32,2,1024,1]{1,0,2,4,3:T(4,128)(2,1)S(1)} %copy.139), kind=kOutput, calls=%fused_computation.14 | convolution fusion | flops 4259840 | bytes 1638400 | tf_op jit(solution)/shard_map/iwcf,ejwcf->eijf/dot_general | solution.py:79
  78.9 4.1 %copy.133 = bf16[2,4,4,1024]{3,2,1,0:T(4,128)(2,1)} copy(bf16[2,4,4,1024]{1,2,0,3:T(4,128)(2,1)} %fusion.11) | data formatting | bytes 131072
  83.0 1.1 %slice_negate_fusion = (bf16[4,32,1,1024]{3,1,2,0:T(8,128)(2,1)S(1)}, bf16[4,32,1,1024]{3,1,2,0:T(8,128)(2,1)S(1)}) fusion(bf16[4,32,2,1024]{3,1,2,0:T(8,128)(2,1)} %collective-permute-done.3), kind=kLoop, calls=%fused_computation.46 | loop fusion | flops 131072 | bytes 1048576 | tf_op jit(solution)/shard_map/neg | solution.py:77
  84.1 1.1 %pad_maximum_fusion.2 = bf16[2,4,32,2,1024]{4,2,3,1,0:T(8,128)(2,1)S(1)} fusion(bf16[1,4,32,2,1024]{4,2,3,1,0:T(8,128)(2,1)S(1)} %maximum_bitcast_fusion.3, bf16[1,4,32,2,1024]{4,2,3,1,0:T(8,128)(2,1)} %bitcast.31), kind=kLoop, calls=%fused_computation.27 | loop fusion | flops 524288 | bytes 2097152 | tf_op jit(solution)/shard_map/stack | solution.py:78
  85.3 5.4 %copy.130 = bf16[2,4,32,2,1024]{2,1,3,0,4:T(4,128)(2,1)} copy(bf16[2,4,32,2,1024]{4,2,3,1,0:T(8,128)(2,1)S(1)} %pad_maximum_fusion.2) | data formatting | bytes 2097152 | tf_op jit(solution)/shard_map/stack | solution.py:78
  90.7 7.0 %fusion.12 = bf16[2,4,4,1024]{1,2,0,3:T(4,128)(2,1)} fusion(bf16[2,4,32,2,1024]{2,1,3,0,4:T(4,128)(2,1)} %copy.130, bf16[4,32,2,1024,1]{1,0,2,4,3:T(4,128)(2,1)S(1)} %copy.139), kind=kOutput, calls=%fused_computation.15 | convolution fusion | flops 4259840 | bytes 1638400 | tf_op jit(solution)/shard_map/iwcf,ejwcf->eijf/dot_general | solution.py:79
  97.7 4.1 %copy.134 = bf16[2,4,4,1024]{3,2,1,0:T(4,128)(2,1)} copy(bf16[2,4,4,1024]{1,2,0,3:T(4,128)(2,1)} %fusion.12) | data formatting | bytes 131072
  (13 shorter events, 0.3 us)
Async XLA Ops:
  3.4 8.6 %copy-start.1 = (s32[4,32]{1,0:T(4,128)S(1)}, s32[4,32]{1,0:T(4,128)}, u32[]{:S(2)}) copy-start(s32[4,32]{1,0:T(4,128)} %param.4) | copy-start | bytes 1540
  5.8 26.3 %copy-start.2 = (f32[1024]{0:T(1024)S(1)}, f32[1024]{0:T(1024)}, u32[]{:S(2)}) copy-start(f32[1024]{0:T(1024)} %param.5) | copy-start | bytes 12292
  5.8 16.3 %all-to-all-start = ((bf16[4,4,2,8,1024]{4,2,1,0,3:T(2,128)(2,1)}), bf16[4,4,2,8,1024]{4,2,1,0,3:T(2,128)(2,1)S(1)}, u32[]{:S(2)}, u32[]{:S(2)}) async-start(bf16[4,4,2,8,1024]{4,2,1,0,3:T(2,128)(2,1)} %copy.117), calls=%async_computation | async-start | bytes 1048576 | tf_op jit(solution)/shard_map/all_to_all | solution.py:89
  23.2 4.3 %collective-permute-start = (f32[4,64]{0,1:T(8,128)S(1)}, f32[4,64]{0,1:T(8,128)S(1)}, u32[]{:S(2)}, u32[]{:S(2)}) collective-permute-start(f32[4,64]{0,1:T(8,128)S(1)} %copy.156), channel_id=1, source_target_pairs={{0,1},{1,2},{2,3},{3,4},{4,5},{5,6},{6,7},{8,9},{9,10},{10,11},{11... | collective-permute-start | bytes 3080 | tf_op jit(solution)/shard_map/ppermute | solution.py:24
  26.1 5.8 %collective-permute-start.1 = (f32[4,64]{0,1:T(8,128)S(1)}, f32[4,64]{0,1:T(8,128)S(1)}, u32[]{:S(2)}, u32[]{:S(2)}) collective-permute-start(f32[4,64]{0,1:T(8,128)S(1)} %copy.157), channel_id=1, source_target_pairs={{1,0},{2,1},{3,2},{4,3},{5,4},{6,5},{7,6},{9,8},{10,9},{11,10},{12... | collective-permute-start | bytes 3080 | tf_op jit(solution)/shard_map/ppermute | solution.py:26
  35.3 29.3 %collective-permute-start.2 = (bf16[4,32,2,1024]{3,1,2,0:T(8,128)(2,1)}, bf16[4,32,2,1024]{3,1,2,0:T(8,128)(2,1)S(1)}, u32[]{:S(2)}, u32[]{:S(2)}) collective-permute-start(bf16[4,32,2,1024]{3,1,2,0:T(8,128)(2,1)} %multiply_convert_fusion), channel_id=1, source_target_pairs={{64,0},{72,8},{80,16},{88,24},{96,32},{104,40},{112,48},{120,56},{... | collective-permute-start | bytes 1572872 | tf_op jit(solution)/shard_map/ppermute | solution.py:36
  38.5 44.5 %collective-permute-start.3 = (bf16[4,32,2,1024]{3,1,2,0:T(8,128)(2,1)}, bf16[4,32,2,1024]{3,1,2,0:T(8,128)(2,1)}, u32[]{:S(2)}, u32[]{:S(2)}) collective-permute-start(bf16[4,32,2,1024]{3,1,2,0:T(8,128)(2,1)} %multiply_convert_fusion), channel_id=1, source_target_pairs={{128,0},{136,8},{144,16},{152,24},{160,32},{168,40},{176,48},{184,... | collective-permute-start | bytes 1572872 | tf_op jit(solution)/shard_map/ppermute | solution.py:36
  64.6 0.8 copy-start
where the time goes:
time: 103 us; the launch traced here: 102 us
  local copies, waits for them, and re-layouts  34.2 us (33%)
  matrix products  22.5 us (22%)
  waiting for transfers between devices  18 us (17%)
  starting transfers between devices  17.7 us (17%)
  other arithmetic  8.45 us (8%)
    dot_general x3, matrix products, cross_spectra(): jnp.einsum('iwcf,ejwcf->eijf', left, stacked, preferred_element_type=jnp....  21 us
    another operation x3, local copies, waits for them, and re-layouts, cross_spectra(): stacked = jnp.stack([right, turned], axis=0)  16.2 us
    unnamed x11, local copies, waits for them, and re-layouts  13.1 us
    all_to_all x1, waiting for transfers between devices, local(): lax.all_to_all(outgoing, 'band', split_axis=3, concat_axis=1, tiled=True)  10.1 us
    ppermute x2, starting transfers between devices, passed_along(): return lax.ppermute(block, axis, route)  7.47 us
    all_to_all x1, starting transfers between devices, local(): lax.all_to_all(outgoing, 'band', split_axis=3, concat_axis=1, tiled=True)  6.24 us
    ppermute x1, waiting for transfers between devices, padded(): lax.ppermute(head, axis, [((i + 1) % count, i) for i in range(ends)])  4.24 us
    ppermute x2, waiting for transfers between devices, passed_along(): return lax.ppermute(block, axis, route)  3.46 us
  transfers between devices with their start and end apart: 5, of which 4 were waited for; matrix products, arithmetic and copies ran while one was open for 36% of the time, Pallas kernels for 0%

commit v1 on v0

v1 whole, which is shorter than its diff:
```python
import math

import jax
import jax.numpy as jnp
import ml_dtypes
import numpy as np
from jax import lax
from jax.experimental import pallas as pl
from jax.experimental.pallas import tpu as pltpu
from jax.sharding import PartitionSpec as P

ROOT = 128
SMOOTH = 64
HALVES = 2
ROWS = 8
epsilon = 1e-06
full_turn = 2.0 * math.pi


def make_tables(bands):
    indices = np.arange(ROOT)
    angles = (indices[:, None] * indices[None, :] % ROOT) * (full_turn / ROOT)
    first = np.concatenate([np.cos(angles), -np.sin(angles)], axis=0)
    twist = (indices[:, None] * indices[None, :]) * (full_turn / (ROOT * ROOT))
    half = angles[: ROOT // 2]
    parts = np.stack(
        [
            np.concatenate([np.cos(half), np.sin(half)], axis=1),
            np.concatenate([-np.sin(half), np.cos(half)], axis=1),
        ],
        axis=0,
    )
    second = parts.reshape(2, bands, ROWS, 2 * ROOT).transpose(1, 0, 2, 3).reshape(ROOT, 2 * ROOT)
    return (
        first.astype(ml_dtypes.bfloat16),
        np.cos(twist).astype(np.float32),
        np.sin(twist).astype(np.float32),
        second.astype(ml_dtypes.bfloat16),
    )


def split_three(values):
    high = values.astype(jnp.bfloat16)
    rest = values - high.astype(jnp.float32)
    middle = rest.astype(jnp.bfloat16)
    low = (rest - middle.astype(jnp.float32)).astype(jnp.bfloat16)
    return high, middle, low


def kernel(
    stations, windows, bands, n_sta,
    x_ref, flag_ref, response_ref, first_ref, cos_ref, sin_ref, second_ref,
    own_ref, near_ref, far_ref,
    xf, tx, rx, before, after, own_acc, near_acc, far_acc, power_ext,
    halo_out, halo_in, scale_own, scale_before, scale_after, stage, far_out,
    tx_send, tx_recv, down_send, down_recv, up_send, up_recv,
    halo_send, halo_recv, scale_send, scale_recv, far_send, far_recv,
):
    me = lax.axis_index("band")
    place = lax.axis_index("sta")
    offset = n_sta // 8
    up = lax.rem(place + offset, n_sta)
    down = lax.rem(place + n_sta - offset, n_sta)
    pair = windows // HALVES

    def peer(order):
        step = order // 2
        bit0 = (me % 2 + order % 2) % 2
        bit1 = ((me // 2) % 2 + step % 2 + step // 2) % 2
        bit2 = (me // 4 + step // 2) % 2
        return bit0 + 2 * bit1 + 4 * bit2

    barrier = pltpu.get_barrier_semaphore()
    for order in range(1, bands):
        pl.semaphore_signal(barrier, inc=1, device_id={"band": peer(order)})
    for other in (up, down):
        pl.semaphore_signal(barrier, inc=1, device_id={"sta": other})

    def send_band(half, order):
        return pltpu.make_async_remote_copy(
            src_ref=tx.at[peer(order), half],
            dst_ref=rx.at[me, half],
            send_sem=tx_send.at[half, order],
            recv_sem=tx_recv.at[half, order],
            device_id={"band": peer(order)},
        )

    def arrival(half, order):
        return pltpu.make_async_remote_copy(
            src_ref=tx.at[peer(order), half],
            dst_ref=rx.at[peer(order), half],
            send_sem=tx_send.at[half, order],
            recv_sem=tx_recv.at[half, order],
            device_id={"band": peer(order)},
        )

    def send_down(half, order):
        return pltpu.make_async_remote_copy(
            src_ref=rx.at[peer(order), half],
            dst_ref=after.at[peer(order), half],
            send_sem=down_send.at[half, order],
            recv_sem=down_recv.at[half, order],
            device_id={"sta": down},
        )

    def send_up(half, order):
        return pltpu.make_async_remote_copy(
            src_ref=rx.at[peer(order), half],
            dst_ref=before.at[peer(order), half],
            send_sem=up_send.at[half, order],
            recv_sem=up_recv.at[half, order],
            device_id={"sta": up},
        )

    def load(buffer, source, half, station, window):
        block = buffer[source, half, station, window].astype(jnp.float32)
        return block[:ROWS], block[ROWS:]

    def add_own(half, order):
        source = peer(order)
        totals = [own_acc[n] for n in range(stations * stations)]
        for window in range(pair):
            parts = [load(rx, source, half, s, window) for s in range(stations)]
            for i in range(stations):
                re_i, im_i = parts[i]
                totals[i * stations + i] += re_i * re_i + im_i * im_i
                for j in range(i + 1, stations):
                    re_j, im_j = parts[j]
                    totals[i * stations + j] += re_i * re_j + im_i * im_j
                    totals[j * stations + i] += im_i * re_j - re_i * im_j
        for n in range(stations * stations):
            own_acc[n] = totals[n]

    def add_cross(acc, left, right, half, order):
        source = peer(order)
        totals = [acc[n] for n in range(2 * stations * stations)]
        for window in range(pair):
            lefts = [load(left, source, half, s, window) for s in range(stations)]
            rights = [load(right, source, half, s, window) for s in range(stations)]
            for i in range(stations):
                re_i, im_i = lefts[i]
                for j in range(stations):
                    re_j, im_j = rights[j]
                    n = i * stations + j
                    totals[n] += re_i * re_j + im_i * im_j
                    totals[stations * stations + n] += im_i * re_j - re_i * im_j
        for n in range(2 * stations * stations):
            acc[n] = totals[n]

    for acc in (own_acc, near_acc, far_acc):
        acc[...] = jnp.zeros_like(acc)

    def unfold(station, carry):
        xf[station] = x_ref[station].astype(jnp.float32)
        return carry

    lax.fori_loop(0, stations, unfold, 0)

    for half in range(HALVES):

        def transform(station, carry):
            columns = [
                xf[station, pl.ds(half * pair + w, ROOT, stride=windows), :].astype(jnp.bfloat16)
                for w in range(pair)
            ]
            section = jnp.dot(
                first_ref[...], jnp.concatenate(columns, axis=1), preferred_element_type=jnp.float32
            )
            twisted = []
            for w in range(pair):
                real_one = section[:ROOT, w * ROOT : (w + 1) * ROOT]
                imag_one = section[ROOT:, w * ROOT : (w + 1) * ROOT]
                real_two = real_one * cos_ref[...] + imag_one * sin_ref[...]
                imag_two = imag_one * cos_ref[...] - real_one * sin_ref[...]
                twisted.append(
                    jnp.concatenate(
                        [real_two.astype(jnp.bfloat16), imag_two.astype(jnp.bfloat16)], axis=1
                    )
                )
            result = lax.dot_general(
                second_ref[...],
                jnp.concatenate(twisted, axis=0),
                (((1,), (1,)), ((), ())),
                preferred_element_type=jnp.float32,
            )
            for w in range(pair):
                gate = flag_ref[station, me * windows + half * pair + w].astype(jnp.float32)
                spectrum = (result[:, w * ROOT : (w + 1) * ROOT] * gate).astype(jnp.bfloat16)
                tx[:, half, station, w] = spectrum.reshape(bands, 2 * ROWS, ROOT)
            return carry

        lax.fori_loop(0, stations, transform, 0)
        rx[me, half] = tx[me, half]
        if half == 0:
            pl.semaphore_wait(barrier, bands + 1)
        send_down(half, 0).start()
        send_up(half, 0).start()
        for order in range(1, bands):
            send_band(half, order).start()

    for half in range(HALVES):
        add_own(half, 0)

        def regroup(order, carry):
            arrival(half, order).wait_recv()
            send_down(half, order).start()
            send_up(half, order).start()
            add_own(half, order)
            return carry

        lax.fori_loop(1, bands, regroup, 0)

    halo_out[...] = jnp.zeros_like(halo_out)
    for s in range(stations):
        power = own_acc[s * stations + s]
        power_ext[s, ROWS : 2 * ROWS] = power
        halo_out[0, s : s + 1] = power[:1]
        halo_out[1, s : s + 1] = power[ROWS - 1 :]

    previous = lax.rem(me + bands - 1, bands)
    following = lax.rem(me + 1, bands)
    halos = [
        pltpu.make_async_remote_copy(
            src_ref=halo_out.at[side],
            dst_ref=halo_in.at[side],
            send_sem=halo_send.at[side],
            recv_sem=halo_recv.at[side],
            device_id={"band": target},
        )
        for side, target in ((0, previous), (1, following))
    ]
    for copy in halos:
        copy.start()

    def crosses(half, order):
        send_down(half, order).wait_recv()
        add_cross(near_acc, rx, after, half, order)
        send_up(half, order).wait_recv()
        add_cross(far_acc, before, after, half, order)

    def partners_first(order, carry):
        crosses(0, order)
        return carry

    def partners_second(order, carry):
        crosses(1, order)
        return carry

    lax.fori_loop(0, bands, partners_first, 0)

    for copy in halos:
        copy.wait_recv()
    next_rows = halo_in[0]
    last_rows = halo_in[1]
    next_rows = jnp.where(me == bands - 1, jnp.zeros_like(next_rows), next_rows)
    last_rows = jnp.where(me == 0, jnp.zeros_like(last_rows), last_rows)
    for s in range(stations):
        power_ext[s, ROWS - 1 : ROWS] = last_rows[s : s + 1]
        power_ext[s, 2 * ROWS : 2 * ROWS + 1] = next_rows[s : s + 1]
    shifted = jnp.concatenate(
        [
            jnp.concatenate(
                [power_ext[s, ROWS - 1 + shift : 2 * ROWS - 1 + shift] for s in range(stations)], axis=0
            )
            for shift in range(3)
        ],
        axis=1,
    )
    sources = lax.broadcasted_iota(jnp.int32, (3 * ROOT, ROOT), 0) - ROOT
    targets = lax.broadcasted_iota(jnp.int32, (3 * ROOT, ROOT), 1)
    distance = sources - targets
    near_enough = ((distance >= -SMOOTH) & (distance <= SMOOTH)).astype(jnp.float32)
    smooth_table = near_enough.astype(jnp.bfloat16)
    summed = jnp.zeros((stations * ROWS, ROOT), jnp.float32)
    for piece in split_three(shifted)[::-1]:
        summed += jnp.dot(piece, smooth_table, preferred_element_type=jnp.float32)
    smooth = summed / ((2 * SMOOTH + 1) * windows * bands)
    root = jnp.sqrt(smooth + epsilon)
    for s in range(stations):
        scale_own[s] = response_ref[...] / root[s * ROWS : (s + 1) * ROWS]

    scales = [
        pltpu.make_async_remote_copy(
            src_ref=scale_own,
            dst_ref=landing,
            send_sem=scale_send.at[side],
            recv_sem=scale_recv.at[side],
            device_id={"sta": target},
        )
        for side, landing, target in ((0, scale_after, down), (1, scale_before, up))
    ]
    for copy in scales:
        copy.start()

    lax.fori_loop(0, bands, partners_second, 0)

    for copy in scales:
        copy.wait_recv()

    share = 1.0 / (windows * bands)
    square = stations * stations

    def finish(target, values, left, right):
        for i in range(stations):
            for e in range(2):
                for j in range(stations):
                    value = values(e, i, j) * (left[i] * right[j] * share)
                    stage[e, i, pl.ds(j, ROWS, stride=stations), :] = value
                target[e, i] = stage[e, i].astype(jnp.bfloat16)

    finish(far_out, lambda e, i, j: far_acc[e * square + i * stations + j], scale_before, scale_after)
    far_copy = pltpu.make_async_remote_copy(
        src_ref=far_out,
        dst_ref=far_ref,
        send_sem=far_send,
        recv_sem=far_recv,
        device_id={"sta": down},
    )
    far_copy.start()

    finish(near_ref, lambda e, i, j: near_acc[e * square + i * stations + j], scale_own, scale_after)

    def own_value(e, i, j):
        low, high = min(i, j), max(i, j)
        if e == 0:
            return own_acc[low * stations + high]
        if i == j:
            return jnp.zeros((ROWS, ROOT), jnp.float32)
        value = own_acc[high * stations + low]
        return value if i < j else -value

    finish(own_ref, own_value, scale_own, scale_own)

    for half in range(HALVES):

        def drain(order, carry):
            send_band(half, order).wait_send()
            return carry

        def drain_partners(order, carry):
            send_down(half, order).wait_send()
            send_up(half, order).wait_send()
            return carry

        lax.fori_loop(1, bands, drain, 0)
        lax.fori_loop(0, bands, drain_partners, 0)
    for copy in halos:
        copy.wait_send()
    for copy in scales:
        copy.wait_send()
    far_copy.wait_send()
    far_copy.wait_recv()


def solution(mesh):
    bands = mesh.shape["band"]
    n_sta = mesh.shape["sta"]
    tables = make_tables(bands)

    def local(traces, live_flag, response):
        stations, windows = traces.shape[0], traces.shape[1]
        folded = traces.reshape(stations, windows, ROOT, ROOT).transpose(0, 2, 1, 3)
        folded = folded.reshape(stations, ROOT * windows, ROOT)
        pair = windows // HALVES
        chunks = (bands, HALVES, stations, pair, 2 * ROWS, ROOT)
        tile = (ROWS, ROOT)
        result = jax.ShapeDtypeStruct((2, stations, ROWS * stations, ROOT), jnp.bfloat16)
        vmem = pl.BlockSpec(memory_space=pltpu.VMEM)

        def body(*refs):
            kernel(stations, windows, bands, n_sta, *refs)

        outs = pl.pallas_call(
            body,
            out_shape=(result, result, result),
            in_specs=[vmem, pl.BlockSpec(memory_space=pltpu.SMEM)] + [vmem] * 5,
            out_specs=(vmem, vmem, vmem),
            scratch_shapes=[
                pltpu.VMEM((stations, ROOT * windows, ROOT), jnp.float32),
                pltpu.VMEM(chunks, jnp.bfloat16),
                pltpu.VMEM(chunks, jnp.bfloat16),
                pltpu.VMEM(chunks, jnp.bfloat16),
                pltpu.VMEM(chunks, jnp.bfloat16),
                pltpu.VMEM((stations * stations,) + tile, jnp.float32),
                pltpu.VMEM((2 * stations * stations,) + tile, jnp.float32),
                pltpu.VMEM((2 * stations * stations,) + tile, jnp.float32),
                pltpu.VMEM((stations, 3 * ROWS, ROOT), jnp.float32),
                pltpu.VMEM((2,) + tile, jnp.float32),
                pltpu.VMEM((2,) + tile, jnp.float32),
                pltpu.VMEM((stations,) + tile, jnp.float32),
                pltpu.VMEM((stations,) + tile, jnp.float32),
                pltpu.VMEM((stations,) + tile, jnp.float32),
                pltpu.VMEM((2, stations, ROWS * stations, ROOT), jnp.float32),
                pltpu.VMEM((2, stations, ROWS * stations, ROOT), jnp.bfloat16),
            ]
            + [pltpu.SemaphoreType.DMA((HALVES, bands))] * 6
            + [pltpu.SemaphoreType.DMA((2,))] * 4
            + [pltpu.SemaphoreType.DMA] * 2,
            compiler_params=pltpu.CompilerParams(
                collective_id=0, has_side_effects=True, vmem_limit_bytes=32 * 1024 * 1024
            ),
        )(folded, live_flag, response.reshape(ROWS, ROOT), *tables)

        def unfold(out):
            split = out.reshape(2, stations, ROWS, stations, ROOT).transpose(0, 1, 3, 2, 4)
            return split.reshape(2, stations, stations, ROWS * ROOT)

        return tuple(unfold(out) for out in outs)

    in_specs = (P("sta", "band", None), P("sta", None), P("band"))
    out_specs = (P(None, "sta", None, "band"),) * 3
    return jax.shard_map(local, mesh=mesh, in_specs=in_specs, out_specs=out_specs, check_vma=False)
```

time: 103 us -> 36.3 us (0.35)
  the two profiles are of different devices: /device:TPU:56 before, /device:TPU:16 now
where the time goes in v1:
time: 36.3 us; the launch traced here: 35.9 us
  Pallas kernels  27.6 us (76%)
  local copies, waits for them, and re-layouts  7.65 us (21%)
  between operations  0.65 us (2%)
    pallas_call x1, Pallas kernels, local(): pl.pallas_call(body, out_shape=(result, result, result), in_specs=[vmem,...  27.6 us
    unnamed x17, local copies, waits for them, and re-layouts  7.65 us

profile of v1, /device:TPU:16, one launch (start us, length us, event | category | flops | bytes accessed | tf_op | source)
XLA Modules:
  0.0 35.9 jit_solution(905982492823343026)
XLA Ops:
  0.6 0.0 copy-start.6
  0.6 0.7 %copy-done.6 = s32[4,32]{1,0:T(4,128)S(1)} copy-done((s32[4,32]{1,0:T(4,128)S(1)}, s32[4,32]{1,0:T(4,128)}, u32[]{:S(2)}) %copy-start.6) | copy-done | bytes 536
  1.3 0.0 copy-start
  1.3 1.0 %copy-done = bf16[4,4,16384]{2,1,0:T(4,128)(2,1)S(1)} copy-done((bf16[4,4,16384]{2,1,0:T(4,128)(2,1)S(1)}, bf16[4,4,16384]{2,1,0:T(4,128)(2,1)}, u32[]{:S(2)}) %copy-start) | copy-done | bytes 524312
  2.4 0.0 copy-start.1
  2.4 0.8 %copy-done.1 = bf16[128,256]{1,0:T(8,128)(2,1)S(1)} copy-done((bf16[128,256]{1,0:T(8,128)(2,1)S(1)}, bf16[128,256]{1,0:T(8,128)(2,1)}, u32[]{:S(2)}) %copy-start.1) | copy-done | bytes 65560
  3.2 0.0 copy-start.2
  3.2 0.8 %copy-done.2 = f32[128,128]{1,0:T(8,128)S(1)} copy-done((f32[128,128]{1,0:T(8,128)S(1)}, f32[128,128]{1,0:T(8,128)}, u32[]{:S(2)}) %copy-start.2) | copy-done | bytes 65560
  4.0 0.0 copy-start.3
  4.0 0.8 %copy-done.3 = f32[128,128]{1,0:T(8,128)S(1)} copy-done((f32[128,128]{1,0:T(8,128)S(1)}, f32[128,128]{1,0:T(8,128)}, u32[]{:S(2)}) %copy-start.3) | copy-done | bytes 65560
  4.9 0.0 copy-start.4
  4.9 0.8 %copy-done.4 = bf16[256,128]{1,0:T(8,128)(2,1)S(1)} copy-done((bf16[256,128]{1,0:T(8,128)(2,1)S(1)}, bf16[256,128]{1,0:T(8,128)(2,1)}, u32[]{:S(2)}) %copy-start.4) | copy-done | bytes 65560
  5.7 0.0 copy-start.5
  5.7 0.7 %copy-done.5 = f32[1024]{0:T(1024)S(1)} copy-done((f32[1024]{0:T(1024)S(1)}, f32[1024]{0:T(1024)}, u32[]{:S(2)}) %copy-start.5) | copy-done | bytes 4120
  6.4 27.6 %shard_map.94 = (bf16[2,4,32,128]{3,2,1,0:T(8,128)(2,1)S(1)}, bf16[2,4,32,128]{3,2,1,0:T(8,128)(2,1)S(1)}, bf16[2,4,32,128]{3,2,1,0:T(8,128)(2,1)S(1)}) custom-call(bf16[4,512,128]{2,1,0:T(8,128)(2,1)S(1)} %bitcast.21, s32[4,32]{1,0:T(4,128)S(1)} %copy-done.6, f32[8,128]{1,0:T(8,128)S(1)} %bitcast.25, bf16[256,128]{1,0:T(8,128)(2,1)S(1)} %copy-done.4, ...), custom_call_target="tpu_custom_call" | custom-call | tf_op jit(solution)/shard_map/pallas_call | solution.py:373
  34.0 0.6 %copy.17 = bf16[2,4,4,1024]{3,2,1,0:T(4,128)(2,1)} copy(bf16[2,4,4,1024]{3,2,1,0:T(4,128)(2,1)S(1)} %bitcast.24) | data formatting | bytes 131072
  34.6 0.6 %copy.18 = bf16[2,4,4,1024]{3,2,1,0:T(4,128)(2,1)} copy(bf16[2,4,4,1024]{3,2,1,0:T(4,128)(2,1)S(1)} %bitcast.23) | data formatting | bytes 131072
  35.2 0.6 %copy.19 = bf16[2,4,4,1024]{3,2,1,0:T(4,128)(2,1)} copy(bf16[2,4,4,1024]{3,2,1,0:T(4,128)(2,1)S(1)} %bitcast.22) | data formatting | bytes 131072
Async XLA Ops:
  0.6 0.7 %copy-start.6 = (s32[4,32]{1,0:T(4,128)S(1)}, s32[4,32]{1,0:T(4,128)}, u32[]{:S(2)}) copy-start(s32[4,32]{1,0:T(4,128)} %refs_1_.1) | copy-start | bytes 1540
  1.3 1.0 %copy-start = (bf16[4,4,16384]{2,1,0:T(4,128)(2,1)S(1)}, bf16[4,4,16384]{2,1,0:T(4,128)(2,1)}, u32[]{:S(2)}) copy-start(bf16[4,4,16384]{2,1,0:T(4,128)(2,1)} %param.7) | copy-start | bytes 1572868
  2.4 0.8 %copy-start.1 = (bf16[128,256]{1,0:T(8,128)(2,1)S(1)}, bf16[128,256]{1,0:T(8,128)(2,1)}, u32[]{:S(2)}) copy-start(bf16[128,256]{1,0:T(8,128)(2,1)} %constant.11.clone.refs_6_) | copy-start | bytes 196612
  3.2 0.8 %copy-start.2 = (f32[128,128]{1,0:T(8,128)S(1)}, f32[128,128]{1,0:T(8,128)}, u32[]{:S(2)}) copy-start(f32[128,128]{1,0:T(8,128)} %constant.10.clone.refs_5_) | copy-start | bytes 196612
  4.0 0.8 %copy-start.3 = (f32[128,128]{1,0:T(8,128)S(1)}, f32[128,128]{1,0:T(8,128)}, u32[]{:S(2)}) copy-start(f32[128,128]{1,0:T(8,128)} %constant.9.clone.refs_4_) | copy-start | bytes 196612
  4.9 0.8 %copy-start.4 = (bf16[256,128]{1,0:T(8,128)(2,1)S(1)}, bf16[256,128]{1,0:T(8,128)(2,1)}, u32[]{:S(2)}) copy-start(bf16[256,128]{1,0:T(8,128)(2,1)} %constant.8.clone.refs_3_) | copy-start | bytes 196612
  5.7 0.7 %copy-start.5 = (f32[1024]{0:T(1024)S(1)}, f32[1024]{0:T(1024)}, u32[]{:S(2)}) copy-start(f32[1024]{0:T(1024)} %param.9) | copy-start | bytes 12292

commit v2 on v1

--- a/solution.py
+++ b/solution.py
@@ -12,6 +12,7 @@
 ROOT = 128
 SMOOTH = 64
 HALVES = 2
+LAG = 8
 ROWS = 8
 epsilon = 1e-06
 full_turn = 2.0 * math.pi
@@ -49,12 +50,13 @@
 
 def kernel(
     stations, windows, bands, n_sta,
+    x_hbm, flag_hbm, response_hbm, first_hbm, cos_hbm, sin_hbm, second_hbm,
+    own_ref, near_ref, far_ref,
     x_ref, flag_ref, response_ref, first_ref, cos_ref, sin_ref, second_ref,
-    own_ref, near_ref, far_ref,
     xf, tx, rx, before, after, own_acc, near_acc, far_acc, power_ext,
-    halo_out, halo_in, scale_own, scale_before, scale_after, stage, far_out,
+    power_out, edge_out, edge_in, scale_own, scale_before, scale_after, stage, far_out,
     tx_send, tx_recv, down_send, down_recv, up_send, up_recv,
-    halo_send, halo_recv, scale_send, scale_recv, far_send, far_recv,
+    edge_send, edge_recv, scale_send, scale_recv, far_send, far_recv, load_x, load_rest,
 ):
     me = lax.axis_index("band")
     place = lax.axis_index("sta")
@@ -70,6 +72,17 @@
         bit2 = (me // 4 + step // 2) % 2
         return bit0 + 2 * bit1 + 4 * bit2
 
+    x_copies = [pltpu.make_async_copy(x_hbm.at[s], x_ref.at[s], load_x.at[s]) for s in range(stations)]
+    rest = (
+        (first_hbm, first_ref), (cos_hbm, cos_ref), (sin_hbm, sin_ref), (second_hbm, second_ref),
+        (flag_hbm, flag_ref), (response_hbm, response_ref),
+    )
+    rest_copies = [
+        pltpu.make_async_copy(source, target, load_rest.at[n]) for n, (source, target) in enumerate(rest)
+    ]
+    for copy in x_copies + rest_copies:
+        copy.start()
+
     barrier = pltpu.get_barrier_semaphore()
     for order in range(1, bands):
         pl.semaphore_signal(barrier, inc=1, device_id={"band": peer(order)})
@@ -91,6 +104,24 @@
             dst_ref=rx.at[peer(order), half],
             send_sem=tx_send.at[half, order],
             recv_sem=tx_recv.at[half, order],
+            device_id={"band": peer(order)},
+        )
+
+    def send_edge(order):
+        return pltpu.make_async_remote_copy(
+            src_ref=edge_out.at[peer(order)],
+            dst_ref=edge_in.at[me],
+            send_sem=edge_send.at[order],
+            recv_sem=edge_recv.at[order],
+            device_id={"band": peer(order)},
+        )
+
+    def edge_arrival(order):
+        return pltpu.make_async_remote_copy(
+            src_ref=edge_out.at[peer(order)],
+            dst_ref=edge_in.at[peer(order)],
+            send_sem=edge_send.at[order],
+            recv_sem=edge_recv.at[order],
             device_id={"band": peer(order)},
         )
 
@@ -150,11 +181,11 @@
     for acc in (own_acc, near_acc, far_acc):
         acc[...] = jnp.zeros_like(acc)
 
-    def unfold(station, carry):
-        xf[station] = x_ref[station].astype(jnp.float32)
-        return carry
-
-    lax.fori_loop(0, stations, unfold, 0)
+    for s in range(stations):
+        x_copies[s].wait()
+        xf[s] = x_ref[s].astype(jnp.float32)
+    for copy in rest_copies:
+        copy.wait()
 
     for half in range(HALVES):
 
@@ -183,10 +214,18 @@
                 (((1,), (1,)), ((), ())),
                 preferred_element_type=jnp.float32,
             )
+            powers = jnp.zeros((bands, ROWS, ROOT), jnp.float32)
             for w in range(pair):
                 gate = flag_ref[station, me * windows + half * pair + w].astype(jnp.float32)
                 spectrum = (result[:, w * ROOT : (w + 1) * ROOT] * gate).astype(jnp.bfloat16)
-                tx[:, half, station, w] = spectrum.reshape(bands, 2 * ROWS, ROOT)
+                chunks = spectrum.reshape(bands, 2 * ROWS, ROOT)
+                tx[:, half, station, w] = chunks
+                wide = chunks.astype(jnp.float32)
+                real, imag = wide[:, :ROWS], wide[:, ROWS:]
+                powers += real * real + imag * imag
+            if half > 0:
+                powers += power_out[station]
+            power_out[station] = powers
             return carry
 
         lax.fori_loop(0, stations, transform, 0)
@@ -195,68 +234,65 @@
             pl.semaphore_wait(barrier, bands + 1)
         send_down(half, 0).start()
         send_up(half, 0).start()
+        if half == HALVES - 1:
+            for band in range(bands):
+                for s in range(stations):
+                    power = power_out[s, band]
+                    if band + 1 < bands:
+                        edge_out[band + 1, s : s + 1] = power[ROWS - 1 :]
+                    else:
+                        edge_out[0, s : s + 1] = jnp.zeros((1, ROOT), jnp.float32)
+                    row = stations + s
+                    if band > 0:
+                        edge_out[band - 1, row : row + 1] = power[:1]
+                    else:
+                        edge_out[bands - 1, row : row + 1] = jnp.zeros((1, ROOT), jnp.float32)
+            edge_in[me] = edge_out[me]
         for order in range(1, bands):
+            if half == HALVES - 1:
+                send_edge(order).start()
             send_band(half, order).start()
 
-    for half in range(HALVES):
-        add_own(half, 0)
-
-        def regroup(order, carry):
-            arrival(half, order).wait_recv()
-            send_down(half, order).start()
-            send_up(half, order).start()
-            add_own(half, order)
-            return carry
-
-        lax.fori_loop(1, bands, regroup, 0)
-
-    halo_out[...] = jnp.zeros_like(halo_out)
-    for s in range(stations):
-        power = own_acc[s * stations + s]
-        power_ext[s, ROWS : 2 * ROWS] = power
-        halo_out[0, s : s + 1] = power[:1]
-        halo_out[1, s : s + 1] = power[ROWS - 1 :]
-
-    previous = lax.rem(me + bands - 1, bands)
-    following = lax.rem(me + 1, bands)
-    halos = [
-        pltpu.make_async_remote_copy(
-            src_ref=halo_out.at[side],
-            dst_ref=halo_in.at[side],
-            send_sem=halo_send.at[side],
-            recv_sem=halo_recv.at[side],
-            device_id={"band": target},
-        )
-        for side, target in ((0, previous), (1, following))
-    ]
-    for copy in halos:
-        copy.start()
-
-    def crosses(half, order):
+    def crosses(index):
+        half, order = index // bands, index % bands
         send_down(half, order).wait_recv()
         add_cross(near_acc, rx, after, half, order)
         send_up(half, order).wait_recv()
         add_cross(far_acc, before, after, half, order)
 
-    def partners_first(order, carry):
-        crosses(0, order)
+    def regroup(index):
+        half, order = index // (bands - 1), 1 + index % (bands - 1)
+        arrival(half, order).wait_recv()
+        send_down(half, order).start()
+        send_up(half, order).start()
+        add_own(half, order)
+
+    def regroup_alone(index, carry):
+        regroup(index)
         return carry
 
-    def partners_second(order, carry):
-        crosses(1, order)
+    def regroup_and_cross(index, carry):
+        regroup(index)
+        crosses(index - LAG)
         return carry
 
-    lax.fori_loop(0, bands, partners_first, 0)
-
-    for copy in halos:
-        copy.wait_recv()
-    next_rows = halo_in[0]
-    last_rows = halo_in[1]
-    next_rows = jnp.where(me == bands - 1, jnp.zeros_like(next_rows), next_rows)
-    last_rows = jnp.where(me == 0, jnp.zeros_like(last_rows), last_rows)
+    def cross_alone(index, carry):
+        crosses(index)
+        return carry
+
+    arrivals = HALVES * (bands - 1)
+    for half in range(HALVES):
+        add_own(half, 0)
+    lax.fori_loop(0, LAG, regroup_alone, 0)
+    lax.fori_loop(LAG, arrivals, regroup_and_cross, 0)
+
+    for order in range(1, bands):
+        edge_arrival(order).wait_recv()
+    edges = jnp.sum(edge_in[...], axis=0)
     for s in range(stations):
-        power_ext[s, ROWS - 1 : ROWS] = last_rows[s : s + 1]
-        power_ext[s, 2 * ROWS : 2 * ROWS + 1] = next_rows[s : s + 1]
+        power_ext[s, ROWS - 1 : ROWS] = edges[s : s + 1]
+        power_ext[s, ROWS : 2 * ROWS] = own_acc[s * stations + s]
+        power_ext[s, 2 * ROWS : 2 * ROWS + 1] = edges[stations + s : stations + s + 1]
     shifted = jnp.concatenate(
         [
             jnp.concatenate(
@@ -292,7 +328,7 @@
     for copy in scales:
         copy.start()
 
-    lax.fori_loop(0, bands, partners_second, 0)
+    lax.fori_loop(arrivals - LAG, HALVES * bands, cross_alone, 0)
 
     for copy in scales:
         copy.wait_recv()
@@ -300,25 +336,43 @@
     share = 1.0 / (windows * bands)
     square = stations * stations
 
-    def finish(target, values, left, right):
-        for i in range(stations):
+    def finish(target, values, left, right, rows):
+        for i in rows:
             for e in range(2):
                 for j in range(stations):
                     value = values(e, i, j) * (left[i] * right[j] * share)
                     stage[e, i, pl.ds(j, ROWS, stride=stations), :] = value
                 target[e, i] = stage[e, i].astype(jnp.bfloat16)
 
-    finish(far_out, lambda e, i, j: far_acc[e * square + i * stations + j], scale_before, scale_after)
-    far_copy = pltpu.make_async_remote_copy(
-        src_ref=far_out,
-        dst_ref=far_ref,
-        send_sem=far_send,
-        recv_sem=far_recv,
-        device_id={"sta": down},
+    far_rows = stations // 2
+    far_copies = []
+    for piece in range(2):
+        rows = range(piece * far_rows, (piece + 1) * far_rows)
+        finish(
+            far_out,
+            lambda e, i, j: far_acc[e * square + i * stations + j],
+            scale_before,
+            scale_after,
+            rows,
+        )
+        span = pl.ds(piece * far_rows, far_rows)
+        copy = pltpu.make_async_remote_copy(
+            src_ref=far_out.at[:, span],
+            dst_ref=far_ref.at[:, span],
+            send_sem=far_send.at[piece],
+            recv_sem=far_recv.at[piece],
+            device_id={"sta": down},
+        )
+        copy.start()
+        far_copies.append(copy)
+
+    finish(
+        near_ref,
+        lambda e, i, j: near_acc[e * square + i * stations + j],
+        scale_own,
+        scale_after,
+        range(stations),
     )
-    far_copy.start()
-
-    finish(near_ref, lambda e, i, j: near_acc[e * square + i * stations + j], scale_own, scale_after)
 
     def own_value(e, i, j):
         low, high = min(i, j), max(i, j)
@@ -329,7 +383,7 @@
         value = own_acc[high * stations + low]
         return value if i < j else -value
 
-    finish(own_ref, own_value, scale_own, scale_own)
+    finish(own_ref, own_value, scale_own, scale_own, range(stations))
 
     for half in range(HALVES):
 
@@ -344,12 +398,25 @@
 
         lax.fori_loop(1, bands, drain, 0)
         lax.fori_loop(0, bands, drain_partners, 0)
-    for copy in halos:
-        copy.wait_send()
+    for order in range(1, bands):
+        send_edge(order).wait_send()
     for copy in scales:
         copy.wait_send()
-    far_copy.wait_send()
-    far_copy.wait_recv()
+    for copy in far_copies:
+        copy.wait_send()
+        copy.wait_recv()
+
+
+def write_out(*refs):
+    sources, targets, sems = refs[:3], refs[3:6], refs[6]
+    copies = [
+        pltpu.make_async_copy(source, target, sems.at[n])
+        for n, (source, target) in enumerate(zip(sources, targets))
+    ]
+    for copy in copies:
+        copy.start()
+    for copy in copies:
+        copy.wait()
 
 
 def solution(mesh):
@@ -367,15 +434,23 @@
         result = jax.ShapeDtypeStruct((2, stations, ROWS * stations, ROOT), jnp.bfloat16)
         vmem = pl.BlockSpec(memory_space=pltpu.VMEM)
 
+        operands = (folded, live_flag, response.reshape(ROWS, ROOT)) + tables
+
         def body(*refs):
             kernel(stations, windows, bands, n_sta, *refs)
 
         outs = pl.pallas_call(
             body,
             out_shape=(result, result, result),
-            in_specs=[vmem, pl.BlockSpec(memory_space=pltpu.SMEM)] + [vmem] * 5,
+            in_specs=[pl.BlockSpec(memory_space=pltpu.HBM)] * 7,
             out_specs=(vmem, vmem, vmem),
             scratch_shapes=[
+                pltpu.VMEM((stations, ROOT * windows, ROOT), jnp.bfloat16),
+                pltpu.SMEM(live_flag.shape, jnp.int32),
+                pltpu.VMEM(tile, jnp.float32),
+            ]
+            + [pltpu.VMEM(table.shape, table.dtype) for table in tables]
+            + [
                 pltpu.VMEM((stations, ROOT * windows, ROOT), jnp.float32),
                 pltpu.VMEM(chunks, jnp.bfloat16),
                 pltpu.VMEM(chunks, jnp.bfloat16),
@@ -385,8 +460,9 @@
                 pltpu.VMEM((2 * stations * stations,) + tile, jnp.float32),
                 pltpu.VMEM((2 * stations * stations,) + tile, jnp.float32),
                 pltpu.VMEM((stations, 3 * ROWS, ROOT), jnp.float32),
-                pltpu.VMEM((2,) + tile, jnp.float32),
-                pltpu.VMEM((2,) + tile, jnp.float32),
+                pltpu.VMEM((stations, bands) + tile, jnp.float32),
+                pltpu.VMEM((bands,) + tile, jnp.float32),
+                pltpu.VMEM((bands,) + tile, jnp.float32),
                 pltpu.VMEM((stations,) + tile, jnp.float32),
                 pltpu.VMEM((stations,) + tile, jnp.float32),
                 pltpu.VMEM((stations,) + tile, jnp.float32),
@@ -394,12 +470,21 @@
                 pltpu.VMEM((2, stations, ROWS * stations, ROOT), jnp.bfloat16),
             ]
             + [pltpu.SemaphoreType.DMA((HALVES, bands))] * 6
+            + [pltpu.SemaphoreType.DMA((bands,))] * 2
             + [pltpu.SemaphoreType.DMA((2,))] * 4
-            + [pltpu.SemaphoreType.DMA] * 2,
+            + [pltpu.SemaphoreType.DMA((stations,)), pltpu.SemaphoreType.DMA((6,))],
             compiler_params=pltpu.CompilerParams(
                 collective_id=0, has_side_effects=True, vmem_limit_bytes=32 * 1024 * 1024
             ),
-        )(folded, live_flag, response.reshape(ROWS, ROOT), *tables)
+        )(*(pltpu.with_memory_space_constraint(a, pltpu.HBM) for a in operands))
+
+        outs = pl.pallas_call(
+            write_out,
+            out_shape=(result, result, result),
+            in_specs=[pl.BlockSpec(memory_space=pl.ANY)] * 3,
+            out_specs=(pl.BlockSpec(memory_space=pltpu.HBM),) * 3,
+            scratch_shapes=[pltpu.SemaphoreType.DMA((3,))],
+        )(*(pltpu.with_memory_space_constraint(a, pltpu.VMEM) for a in outs))
 
         def unfold(out):
             split = out.reshape(2, stations, ROWS, stations, ROOT).transpose(0, 1, 3, 2, 4)

time: 36.3 us -> 28.4 us (0.78)
  the two profiles are of different devices: /device:TPU:16 before, /device:TPU:144 now
where the time goes in v2:
time: 28.4 us; the launch traced here: 28.3 us
  Pallas kernels  27.6 us (97%)
  between operations  0.64 us (2%)
    pallas_call x1, Pallas kernels, local(): pl.pallas_call(body, out_shape=(result, result, result), in_specs=[pl.Blo...  26.9 us
    pallas_call x1, Pallas kernels, local(): pl.pallas_call(write_out, out_shape=(result, result, result), in_specs=[p...  0.7 us

profile of v2, /device:TPU:144, one launch (start us, length us, event | category | flops | bytes accessed | tf_op | source)
XLA Modules:
  0.0 28.3 jit_solution(13950635669766342063)
XLA Ops:
  0.6 26.9 %shard_map.94 = (bf16[2,4,32,128]{3,2,1,0:T(8,128)(2,1)S(1)}, bf16[2,4,32,128]{3,2,1,0:T(8,128)(2,1)S(1)}, bf16[2,4,32,128]{3,2,1,0:T(8,128)(2,1)S(1)}) custom-call(bf16[4,512,128]{2,1,0:T(8,128)(2,1)} %bitcast.21, s32[4,32]{1,0:T(4,128)} %refs_1_.1, f32[8,128]{1,0:T(8,128)} %bitcast.22, bf16[256,128]{1,0:T(8,128)(2,1)} %constant.8.clone.refs_3_, ...), custom_call_target="tpu_custom_call" | custom-call | tf_op jit(solution)/shard_map/pallas_call | solution.py:442
  27.6 0.7 %shard_map.95 = (bf16[2,4,32,128]{3,2,1,0:T(8,128)(2,1)}, bf16[2,4,32,128]{3,2,1,0:T(8,128)(2,1)}, bf16[2,4,32,128]{3,2,1,0:T(8,128)(2,1)}) custom-call(bf16[2,4,32,128]{3,2,1,0:T(8,128)(2,1)S(1)} %get-tuple-element.9.refs_0_, bf16[2,4,32,128]{3,2,1,0:T(8,128)(2,1)S(1)} %get-tuple-element.10.refs_1_, bf16[2,4,32,128]{3,2,1,0:T(8,128)(2,1)S(1)} %get-tuple-element.11.refs_2_), custom_call_target="tpu_custom_call" | custom-call | tf_op jit(solution)/shard_map/pallas_call | solution.py:481

commit v3 on v2

--- a/solution.py
+++ b/solution.py
@@ -12,7 +12,7 @@
 ROOT = 128
 SMOOTH = 64
 HALVES = 2
-LAG = 8
+SAME = 4
 ROWS = 8
 epsilon = 1e-06
 full_turn = 2.0 * math.pi
@@ -56,7 +56,7 @@
     xf, tx, rx, before, after, own_acc, near_acc, far_acc, power_ext,
     power_out, edge_out, edge_in, scale_own, scale_before, scale_after, stage, far_out,
     tx_send, tx_recv, down_send, down_recv, up_send, up_recv,
-    edge_send, edge_recv, scale_send, scale_recv, far_send, far_recv, load_x, load_rest,
+    edge_send, edge_recv, scale_send, scale_recv, far_send, far_recv, load_x, load_rest, entered,
 ):
     me = lax.axis_index("band")
     place = lax.axis_index("sta")
@@ -65,12 +65,14 @@
     down = lax.rem(place + n_sta - offset, n_sta)
     pair = windows // HALVES
 
+    bit2 = me % 2
+    bit1 = me // 4
+    bit0 = ((me // 2) % 2 + bit1) % 2
+
     def peer(order):
-        step = order // 2
-        bit0 = (me % 2 + order % 2) % 2
-        bit1 = ((me // 2) % 2 + step % 2 + step // 2) % 2
-        bit2 = (me // 4 + step // 2) % 2
-        return bit0 + 2 * bit1 + 4 * bit2
+        other1 = (bit1 + order // 2) % 2
+        other0 = (bit0 + order) % 2
+        return 4 * other1 + 2 * ((other0 + other1) % 2) + (bit2 + order // 4) % 2
 
     x_copies = [pltpu.make_async_copy(x_hbm.at[s], x_ref.at[s], load_x.at[s]) for s in range(stations)]
     rest = (
@@ -84,10 +86,15 @@
         copy.start()
 
     barrier = pltpu.get_barrier_semaphore()
-    for order in range(1, bands):
-        pl.semaphore_signal(barrier, inc=1, device_id={"band": peer(order)})
     for other in (up, down):
         pl.semaphore_signal(barrier, inc=1, device_id={"sta": other})
+    for order in range(1, SAME):
+        pl.semaphore_signal(barrier, inc=1, device_id={"band": peer(order)})
+
+    @pl.when(bit2 == 0)
+    def _():
+        for order in range(SAME, bands):
+            pl.semaphore_signal(barrier, inc=1, device_id={"band": peer(order)})
 
     def send_band(half, order):
         return pltpu.make_async_remote_copy(
@@ -180,6 +187,12 @@
 
     for acc in (own_acc, near_acc, far_acc):
         acc[...] = jnp.zeros_like(acc)
+
+    @pl.when(bit2 == 1)
+    def _():
+        pl.semaphore_wait(barrier, 1 + 2 * SAME)
+        for order in range(SAME, bands):
+            pl.semaphore_signal(entered.at[order], inc=1, device_id={"band": peer(order)})
 
     for s in range(stations):
         x_copies[s].wait()
@@ -228,10 +241,14 @@
             power_out[station] = powers
             return carry
 
-        lax.fori_loop(0, stations, transform, 0)
+        lax.fori_loop(0, stations, transform, 0, unroll=True)
         rx[me, half] = tx[me, half]
         if half == 0:
-            pl.semaphore_wait(barrier, bands + 1)
+
+            @pl.when(bit2 == 0)
+            def _():
+                pl.semaphore_wait(barrier, 1 + SAME)
+
         send_down(half, 0).start()
         send_up(half, 0).start()
         if half == HALVES - 1:
@@ -248,43 +265,58 @@
                     else:
                         edge_out[bands - 1, row : row + 1] = jnp.zeros((1, ROOT), jnp.float32)
             edge_in[me] = edge_out[me]
-        for order in range(1, bands):
-            if half == HALVES - 1:
+        for order in range(1, SAME):
+            if half > 0:
                 send_edge(order).start()
             send_band(half, order).start()
 
-    def crosses(index):
-        half, order = index // bands, index % bands
+    def send_other():
+        for half in range(HALVES):
+            for order in range(SAME, bands):
+                if half == 0:
+                    send_edge(order).start()
+                send_band(half, order).start()
+
+    @pl.when(bit2 == 1)
+    def _():
+        send_other()
+
+    def crosses(half, order):
         send_down(half, order).wait_recv()
         add_cross(near_acc, rx, after, half, order)
         send_up(half, order).wait_recv()
         add_cross(far_acc, before, after, half, order)
 
-    def regroup(index):
-        half, order = index // (bands - 1), 1 + index % (bands - 1)
+    def regroup(half, order):
         arrival(half, order).wait_recv()
         send_down(half, order).start()
         send_up(half, order).start()
         add_own(half, order)
 
-    def regroup_alone(index, carry):
-        regroup(index)
+    def regroup_same(index, carry):
+        regroup(index // (SAME - 1), 1 + index % (SAME - 1))
         return carry
 
-    def regroup_and_cross(index, carry):
-        regroup(index)
-        crosses(index - LAG)
+    def regroup_other(index, carry):
+        regroup(index // SAME, SAME + index % SAME)
+        crosses(index // SAME, index % SAME)
         return carry
 
-    def cross_alone(index, carry):
-        crosses(index)
+    def cross_other(index, carry):
+        crosses(index // SAME, SAME + index % SAME)
         return carry
 
-    arrivals = HALVES * (bands - 1)
     for half in range(HALVES):
         add_own(half, 0)
-    lax.fori_loop(0, LAG, regroup_alone, 0)
-    lax.fori_loop(LAG, arrivals, regroup_and_cross, 0)
+    @pl.when(bit2 == 0)
+    def _():
+        for order in range(SAME, bands):
+            pl.semaphore_wait(entered.at[order], 1)
+        send_other()
+
+    lax.fori_loop(0, HALVES * (SAME - 1), regroup_same, 0)
+
+    lax.fori_loop(0, HALVES * SAME, regroup_other, 0)
 
     for order in range(1, bands):
         edge_arrival(order).wait_recv()
@@ -328,7 +360,7 @@
     for copy in scales:
         copy.start()
 
-    lax.fori_loop(arrivals - LAG, HALVES * bands, cross_alone, 0)
+    lax.fori_loop(0, HALVES * SAME, cross_other, 0)
 
     for copy in scales:
         copy.wait_recv()
@@ -472,7 +504,8 @@
             + [pltpu.SemaphoreType.DMA((HALVES, bands))] * 6
             + [pltpu.SemaphoreType.DMA((bands,))] * 2
             + [pltpu.SemaphoreType.DMA((2,))] * 4
-            + [pltpu.SemaphoreType.DMA((stations,)), pltpu.SemaphoreType.DMA((6,))],
+            + [pltpu.SemaphoreType.DMA((stations,)), pltpu.SemaphoreType.DMA((6,))]
+            + [pltpu.SemaphoreType.REGULAR((bands,))],
             compiler_params=pltpu.CompilerParams(
                 collective_id=0, has_side_effects=True, vmem_limit_bytes=32 * 1024 * 1024
             ),

time: 28.4 us -> 27.1 us (0.954)
  the two profiles are of different devices: /device:TPU:144 before, /device:TPU:56 now
where the time goes in v3:
time: 27.1 us; the launch traced here: 26.9 us
  Pallas kernels  26.3 us (97%)
  between operations  0.64 us (2%)
    pallas_call x1, Pallas kernels, local(): pl.pallas_call(body, out_shape=(result, result, result), in_specs=[pl.Blo...  25.6 us
    pallas_call x1, Pallas kernels, local(): pl.pallas_call(write_out, out_shape=(result, result, result), in_specs=[p...  0.7 us

profile of v3, /device:TPU:56, one launch (start us, length us, event | category | flops | bytes accessed | tf_op | source)
XLA Modules:
  0.0 26.9 jit_solution(12076474212003918562)
XLA Ops:
  0.6 25.6 %shard_map.94 = (bf16[2,4,32,128]{3,2,1,0:T(8,128)(2,1)S(1)}, bf16[2,4,32,128]{3,2,1,0:T(8,128)(2,1)S(1)}, bf16[2,4,32,128]{3,2,1,0:T(8,128)(2,1)S(1)}) custom-call(bf16[4,512,128]{2,1,0:T(8,128)(2,1)} %bitcast.21, s32[4,32]{1,0:T(4,128)} %refs_1_.1, f32[8,128]{1,0:T(8,128)} %bitcast.22, bf16[256,128]{1,0:T(8,128)(2,1)} %constant.8.clone.refs_3_, ...), custom_call_target="tpu_custom_call" | custom-call | tf_op jit(solution)/shard_map/pallas_call | solution.py:474
  26.2 0.7 %shard_map.95 = (bf16[2,4,32,128]{3,2,1,0:T(8,128)(2,1)}, bf16[2,4,32,128]{3,2,1,0:T(8,128)(2,1)}, bf16[2,4,32,128]{3,2,1,0:T(8,128)(2,1)}) custom-call(bf16[2,4,32,128]{3,2,1,0:T(8,128)(2,1)S(1)} %get-tuple-element.9.refs_0_, bf16[2,4,32,128]{3,2,1,0:T(8,128)(2,1)S(1)} %get-tuple-element.10.refs_1_, bf16[2,4,32,128]{3,2,1,0:T(8,128)(2,1)S(1)} %get-tuple-element.11.refs_2_), custom_call_target="tpu_custom_call" | custom-call | tf_op jit(solution)/shard_map/pallas_call | solution.py:514

commit v4 on v3

--- a/solution.py
+++ b/solution.py
@@ -188,11 +188,16 @@
     for acc in (own_acc, near_acc, far_acc):
         acc[...] = jnp.zeros_like(acc)
 
-    @pl.when(bit2 == 1)
-    def _():
+    def answer():
         pl.semaphore_wait(barrier, 1 + 2 * SAME)
         for order in range(SAME, bands):
             pl.semaphore_signal(entered.at[order], inc=1, device_id={"band": peer(order)})
+
+    first_in = bit1 == 0
+
+    @pl.when((bit2 == 1) & jnp.logical_not(first_in))
+    def _():
+        answer()
 
     for s in range(stations):
         x_copies[s].wait()
@@ -249,6 +254,10 @@
             def _():
                 pl.semaphore_wait(barrier, 1 + SAME)
 
+            @pl.when((bit2 == 1) & first_in)
+            def _():
+                answer()
+
         send_down(half, 0).start()
         send_up(half, 0).start()
         if half == HALVES - 1:
@@ -302,8 +311,15 @@
         crosses(index // SAME, index % SAME)
         return carry
 
-    def cross_other(index, carry):
-        crosses(index // SAME, SAME + index % SAME)
+    def far_other(index, carry):
+        half, order = index // SAME, SAME + index % SAME
+        send_down(half, order).wait_recv()
+        send_up(half, order).wait_recv()
+        add_cross(far_acc, before, after, half, order)
+        return carry
+
+    def near_other(index, carry):
+        add_cross(near_acc, rx, after, index // SAME, SAME + index % SAME)
         return carry
 
     for half in range(HALVES):
@@ -360,7 +376,7 @@
     for copy in scales:
         copy.start()
 
-    lax.fori_loop(0, HALVES * SAME, cross_other, 0)
+    lax.fori_loop(0, HALVES * SAME, far_other, 0)
 
     for copy in scales:
         copy.wait_recv()
@@ -398,6 +414,7 @@
         copy.start()
         far_copies.append(copy)
 
+    lax.fori_loop(0, HALVES * SAME, near_other, 0)
     finish(
         near_ref,
         lambda e, i, j: near_acc[e * square + i * stations + j],

time: 27.1 us -> 27.1 us (level)
  no operation moved by 1% of the time
where the time goes in v4:
time: 27.1 us; the launch traced here: 26.9 us
  Pallas kernels  26.3 us (97%)
  between operations  0.64 us (2%)
    pallas_call x1, Pallas kernels, local(): pl.pallas_call(body, out_shape=(result, result, result), in_specs=[pl.Blo...  25.6 us
    pallas_call x1, Pallas kernels, local(): pl.pallas_call(write_out, out_shape=(result, result, result), in_specs=[p...  0.7 us

profile of v4, /device:TPU:56, one launch (start us, length us, event | category | flops | bytes accessed | tf_op | source)
XLA Modules:
  0.0 26.9 jit_solution(15814609760655251411)
XLA Ops:
  0.6 25.6 %shard_map.94 = (bf16[2,4,32,128]{3,2,1,0:T(8,128)(2,1)S(1)}, bf16[2,4,32,128]{3,2,1,0:T(8,128)(2,1)S(1)}, bf16[2,4,32,128]{3,2,1,0:T(8,128)(2,1)S(1)}) custom-call(bf16[4,512,128]{2,1,0:T(8,128)(2,1)} %bitcast.21, s32[4,32]{1,0:T(4,128)} %refs_1_.1, f32[8,128]{1,0:T(8,128)} %bitcast.22, bf16[256,128]{1,0:T(8,128)(2,1)} %constant.8.clone.refs_3_, ...), custom_call_target="tpu_custom_call" | custom-call | tf_op jit(solution)/shard_map/pallas_call | solution.py:491
  26.2 0.7 %shard_map.95 = (bf16[2,4,32,128]{3,2,1,0:T(8,128)(2,1)}, bf16[2,4,32,128]{3,2,1,0:T(8,128)(2,1)}, bf16[2,4,32,128]{3,2,1,0:T(8,128)(2,1)}) custom-call(bf16[2,4,32,128]{3,2,1,0:T(8,128)(2,1)S(1)} %get-tuple-element.9.refs_0_, bf16[2,4,32,128]{3,2,1,0:T(8,128)(2,1)S(1)} %get-tuple-element.10.refs_1_, bf16[2,4,32,128]{3,2,1,0:T(8,128)(2,1)S(1)} %get-tuple-element.11.refs_2_), custom_call_target="tpu_custom_call" | custom-call | tf_op jit(solution)/shard_map/pallas_call | solution.py:531

commit v5 on v4

--- a/solution.py
+++ b/solution.py
@@ -74,6 +74,17 @@
         other0 = (bit0 + order) % 2
         return 4 * other1 + 2 * ((other0 + other1) % 2) + (bit2 + order // 4) % 2
 
+    barrier = pltpu.get_barrier_semaphore()
+    for other in (up, down):
+        pl.semaphore_signal(barrier, inc=1, device_id={"sta": other})
+    for order in range(1, SAME):
+        pl.semaphore_signal(barrier, inc=1, device_id={"band": peer(order)})
+
+    @pl.when(bit2 == 0)
+    def _():
+        for order in range(SAME, bands):
+            pl.semaphore_signal(barrier, inc=1, device_id={"band": peer(order)})
+
     x_copies = [pltpu.make_async_copy(x_hbm.at[s], x_ref.at[s], load_x.at[s]) for s in range(stations)]
     rest = (
         (first_hbm, first_ref), (cos_hbm, cos_ref), (sin_hbm, sin_ref), (second_hbm, second_ref),
@@ -84,17 +95,6 @@
     ]
     for copy in x_copies + rest_copies:
         copy.start()
-
-    barrier = pltpu.get_barrier_semaphore()
-    for other in (up, down):
-        pl.semaphore_signal(barrier, inc=1, device_id={"sta": other})
-    for order in range(1, SAME):
-        pl.semaphore_signal(barrier, inc=1, device_id={"band": peer(order)})
-
-    @pl.when(bit2 == 0)
-    def _():
-        for order in range(SAME, bands):
-            pl.semaphore_signal(barrier, inc=1, device_id={"band": peer(order)})
 
     def send_band(half, order):
         return pltpu.make_async_remote_copy(

time: 27.1 us -> 27 us (level)
  no operation moved by 1% of the time
where the time goes in v5:
time: 27 us; the launch traced here: 26.9 us
  Pallas kernels  26.3 us (97%)
  between operations  0.64 us (2%)
    pallas_call x1, Pallas kernels, local(): pl.pallas_call(body, out_shape=(result, result, result), in_specs=[pl.Blo...  25.6 us
    pallas_call x1, Pallas kernels, local(): pl.pallas_call(write_out, out_shape=(result, result, result), in_specs=[p...  0.7 us

profile of v5, /device:TPU:56, one launch (start us, length us, event | category | flops | bytes accessed | tf_op | source)
XLA Modules:
  0.0 26.9 jit_solution(10548627870305688020)
XLA Ops:
  0.6 25.6 %shard_map.94 = (bf16[2,4,32,128]{3,2,1,0:T(8,128)(2,1)S(1)}, bf16[2,4,32,128]{3,2,1,0:T(8,128)(2,1)S(1)}, bf16[2,4,32,128]{3,2,1,0:T(8,128)(2,1)S(1)}) custom-call(bf16[4,512,128]{2,1,0:T(8,128)(2,1)} %bitcast.21, s32[4,32]{1,0:T(4,128)} %refs_1_.1, f32[8,128]{1,0:T(8,128)} %bitcast.22, bf16[256,128]{1,0:T(8,128)(2,1)} %constant.8.clone.refs_3_, ...), custom_call_target="tpu_custom_call" | custom-call | tf_op jit(solution)/shard_map/pallas_call | solution.py:491
  26.2 0.7 %shard_map.95 = (bf16[2,4,32,128]{3,2,1,0:T(8,128)(2,1)}, bf16[2,4,32,128]{3,2,1,0:T(8,128)(2,1)}, bf16[2,4,32,128]{3,2,1,0:T(8,128)(2,1)}) custom-call(bf16[2,4,32,128]{3,2,1,0:T(8,128)(2,1)S(1)} %get-tuple-element.9.refs_0_, bf16[2,4,32,128]{3,2,1,0:T(8,128)(2,1)S(1)} %get-tuple-element.10.refs_1_, bf16[2,4,32,128]{3,2,1,0:T(8,128)(2,1)S(1)} %get-tuple-element.11.refs_2_), custom_call_target="tpu_custom_call" | custom-call | tf_op jit(solution)/shard_map/pallas_call | solution.py:531
